TPU v7x, 32 devices: a whole 2x2x4 slice. The times are simulated.
32 devices in a mesh: fsdp: 32 (over z, y, x, core).
Axes of the slice: x: 2, y: 2, z: 4, core: 2. Of those that a mesh axis runs over, the one named last changes fastest.
Arguments:
- tokens: bfloat16 [12608, 768], P('fsdp'), may hold values from -6 to 6
- cotangent: bfloat16 [12608, 768], P('fsdp'), may hold values from -6 to 6
- expert_ids: int32 [12608, 2], P('fsdp'), may hold values from 0 to 3, as said below
- slots: int32 [12608, 2], P('fsdp'), may hold values from 0 to 245, as said below
- norm1_gain: bfloat16 [768], P('fsdp'), may hold values from 0.5 to 1.5
- norm1_shift: bfloat16 [768], P('fsdp'), may hold values from -1.75 to 1.75
- query_weight: bfloat16 [768, 768], P('fsdp'), may hold values from -0.21875 to 0.21875
- query_bias: bfloat16 [768], P('fsdp'), may hold values from -1.75 to 1.75
- key_weight: bfloat16 [768, 768], P('fsdp'), may hold values from -0.21875 to 0.21875
- value_weight: bfloat16 [768, 768], P('fsdp'), may hold values from -0.21875 to 0.21875
- value_bias: bfloat16 [768], P('fsdp'), may hold values from -1.75 to 1.75
- out_weight: bfloat16 [768, 768], P('fsdp'), may hold values from -0.875 to 0.875
- out_bias: bfloat16 [768], P('fsdp'), may hold values from -1.75 to 1.75
- norm2_gain: bfloat16 [768], P('fsdp'), may hold values from 0.5 to 1.5
- norm2_shift: bfloat16 [768], P('fsdp'), may hold values from -1.75 to 1.75
- router_weight: bfloat16 [768, 4], P('fsdp'), may hold values from -0.15625 to 0.15625
- expert_in: bfloat16 [4, 768, 3072], P(None, 'fsdp'), may hold values from -0.21875 to 0.21875
- expert_in_bias: bfloat16 [4, 3072], P(None, 'fsdp'), may hold values from -1.75 to 1.75
- expert_out: bfloat16 [4, 3072, 768], P(None, 'fsdp'), may hold values from -0.109375 to 0.109375
- expert_out_bias: bfloat16 [4, 768], P(None, 'fsdp'), may hold values from -1.75 to 1.75
Outputs:
- mixed_out: bfloat16 [12608, 768], P('fsdp')
- tokens_grad: float32 [12608, 768], P('fsdp')
- norm1_gain_grad: float32 [768], P('fsdp')
- norm1_shift_grad: float32 [768], P('fsdp')
- query_weight_grad: float32 [768, 768], P('fsdp')
- query_bias_grad: float32 [768], P('fsdp')
- key_weight_grad: float32 [768, 768], P('fsdp')
- value_weight_grad: float32 [768, 768], P('fsdp')
- value_bias_grad: float32 [768], P('fsdp')
- out_weight_grad: float32 [768, 768], P('fsdp')
- out_bias_grad: float32 [768], P('fsdp')
- norm2_gain_grad: float32 [768], P('fsdp')
- norm2_shift_grad: float32 [768], P('fsdp')
- router_weight_grad: float32 [768, 4], P('fsdp')
- expert_in_grad: float32 [4, 768, 3072], P(None, 'fsdp')
- expert_in_bias_grad: float32 [4, 3072], P(None, 'fsdp')
- expert_out_grad: float32 [4, 3072, 768], P(None, 'fsdp')
- expert_out_bias_grad: float32 [4, 768], P(None, 'fsdp')
Inputs may be any that keep to these rules, and one draw needn't show every extreme that they name: `expert_ids`: each token's two experts differ. `slots`: among one device's tokens no two choices share both expert and slot, so an expert takes at most 246 of one device's choices; on every device some expert takes exactly 246.
All inputs are finite; a program needn't handle non-finite values.
Results may differ from a plain program's by a relative error of at most 0.029.
Values may be sent and summed in bfloat16 or wider, within the bound.
No kernel may reach another device: no remote copies, remote signals or barrier semaphores. Data moves between devices by JAX's collectives and lax.ppermute only.
A program may use at most 320 MiB of HBM per device.

v0:
```python
import jax
import jax.numpy as jnp
from jax import lax
from jax.sharding import PartitionSpec as P

D = 768
HEADS = 12
HEAD_DIM = 64
EXP = 4
SEQ = 197
CAP = 246


EPSILON = 1e-05
SCALE = 0.125


def norm_rows(values, gain, shift):
    mean_row = jnp.mean(values, -1, keepdims=True)
    centred = values - mean_row
    rstd_row = lax.rsqrt(jnp.mean(centred * centred, -1, keepdims=True) + EPSILON)
    unit_rows = centred * rstd_row
    return (unit_rows * gain + shift, unit_rows, rstd_row)


def norm_back(grad_in, unit_rows, rstd_row, gain):
    scaled = grad_in * gain
    input_grad = rstd_row * (
        scaled
        - jnp.mean(scaled, -1, keepdims=True)
        - unit_rows * jnp.mean(scaled * unit_rows, -1, keepdims=True)
    )
    return (input_grad, jnp.sum(grad_in * unit_rows, 0), jnp.sum(grad_in, 0))


def smooth_gelu(inner):
    return 0.5 * inner * (1.0 + jnp.tanh(0.7978845608 * (inner + 0.044715 * inner * inner * inner)))


def soft_max(values):
    row_max = jnp.max(values, -1, keepdims=True)
    raised = jnp.exp(values - row_max)
    return raised / jnp.sum(raised, -1, keepdims=True)


def per_device(
    tokens,
    cotangent,
    expert_ids,
    slots,
    norm1_gain,
    norm1_shift,
    query_weight,
    query_bias,
    key_weight,
    value_weight,
    value_bias,
    out_weight,
    out_bias,
    norm2_gain,
    norm2_shift,
    router_weight,
    expert_in,
    expert_in_bias,
    expert_out,
    expert_out_bias,
):
    f32 = jnp.float32
    bf16 = jnp.bfloat16
    attn_full = (
        lax.all_gather(norm1_gain, "fsdp", axis=0, tiled=True),
        lax.all_gather(norm1_shift, "fsdp", axis=0, tiled=True),
        lax.all_gather(query_weight, "fsdp", axis=0, tiled=True),
        lax.all_gather(query_bias, "fsdp", axis=0, tiled=True),
        lax.all_gather(key_weight, "fsdp", axis=0, tiled=True),
        lax.all_gather(value_weight, "fsdp", axis=0, tiled=True),
        lax.all_gather(value_bias, "fsdp", axis=0, tiled=True),
        lax.all_gather(out_weight, "fsdp", axis=0, tiled=True),
        lax.all_gather(out_bias, "fsdp", axis=0, tiled=True),
        lax.all_gather(norm2_gain, "fsdp", axis=0, tiled=True),
        lax.all_gather(norm2_shift, "fsdp", axis=0, tiled=True),
        lax.all_gather(router_weight, "fsdp", axis=0, tiled=True),
    )
    expert_full = (
        lax.all_gather(expert_in, "fsdp", axis=1, tiled=True),
        lax.all_gather(expert_in_bias, "fsdp", axis=1, tiled=True),
        lax.all_gather(expert_out, "fsdp", axis=1, tiled=True),
        lax.all_gather(expert_out_bias, "fsdp", axis=1, tiled=True),
    )
    (
        gain_one,
        shift_one,
        w_query,
        b_query,
        w_key,
        w_value,
        b_value,
        w_out,
        b_out,
        gain_two,
        shift_two,
        w_router,
    ) = attn_full
    w_in, b_in, w_exit, b_exit = expert_full
    tok_rows = tokens.shape[0]
    images = tok_rows // SEQ
    heads_shape = (images, SEQ, HEADS, HEAD_DIM)
    inputs = tokens.astype(f32)
    normed_a, unit_a, rstd_a = norm_rows(inputs, gain_one.astype(f32), shift_one.astype(f32))
    hidden_a = normed_a.astype(bf16)
    query = (jnp.dot(hidden_a, w_query, preferred_element_type=f32) + b_query.astype(f32)).astype(
        bf16
    )
    keys_all = jnp.dot(hidden_a, w_key, preferred_element_type=f32).astype(bf16)
    values_all = (
        jnp.dot(hidden_a, w_value, preferred_element_type=f32) + b_value.astype(f32)
    ).astype(bf16)
    query_h = query.reshape(heads_shape)
    key_h = keys_all.reshape(heads_shape)
    value_h = values_all.reshape(heads_shape)
    scores = jnp.einsum("ishd,ithd->ihst", query_h, key_h, preferred_element_type=f32) * SCALE
    row_max = jnp.max(scores, -1, keepdims=True)
    raised = jnp.exp(scores - row_max)
    row_total = jnp.sum(raised, -1, keepdims=True)
    probs = raised / row_total
    log_total = row_max + jnp.log(row_total)
    mixed_h = jnp.einsum("ihst,ithd->ishd", probs.astype(bf16), value_h, preferred_element_type=f32)
    attended = mixed_h.astype(bf16).reshape(tok_rows, D)
    branch_a = jnp.dot(attended, w_out, preferred_element_type=f32) + b_out.astype(f32)
    resid = inputs + branch_a
    normed_b, unit_b, rstd_b = norm_rows(resid, gain_two.astype(f32), shift_two.astype(f32))
    hidden_b = normed_b.astype(bf16)
    logits = jnp.dot(hidden_b, w_router, preferred_element_type=f32)
    one_hot = (expert_ids[:, :, None] == jnp.arange(EXP, dtype=jnp.int32)[None, None, :]).astype(
        f32
    )
    chosen = jnp.einsum("te,tke->tk", logits, one_hot)
    gates = soft_max(chosen)
    cell_index = expert_ids * CAP + slots
    flat_cells = cell_index.reshape(-1)
    blocks = (
        jnp.zeros((EXP * CAP, D), bf16)
        .at[flat_cells]
        .set(jnp.repeat(hidden_b, 2, axis=0))
        .reshape(EXP, CAP, D)
    )
    inner = (
        jnp.einsum("ecd,edf->ecf", blocks, w_in, preferred_element_type=f32)
        + b_in.astype(f32)[:, None, :]
    )
    activ = smooth_gelu(inner).astype(bf16)
    expert_y = (
        jnp.einsum("ecf,efd->ecd", activ, w_exit, preferred_element_type=f32)
        + b_exit.astype(f32)[:, None, :]
    )
    picked = expert_y.reshape(EXP * CAP, D)[cell_index]
    moe_sum = jnp.einsum("tk,tkd->td", gates, picked)
    mixed_out = (resid + moe_sum).astype(bf16)
    attn_back = (
        lax.all_gather(norm1_gain, "fsdp", axis=0, tiled=True),
        lax.all_gather(norm1_shift, "fsdp", axis=0, tiled=True),
        lax.all_gather(query_weight, "fsdp", axis=0, tiled=True),
        lax.all_gather(query_bias, "fsdp", axis=0, tiled=True),
        lax.all_gather(key_weight, "fsdp", axis=0, tiled=True),
        lax.all_gather(value_weight, "fsdp", axis=0, tiled=True),
        lax.all_gather(value_bias, "fsdp", axis=0, tiled=True),
        lax.all_gather(out_weight, "fsdp", axis=0, tiled=True),
        lax.all_gather(out_bias, "fsdp", axis=0, tiled=True),
        lax.all_gather(norm2_gain, "fsdp", axis=0, tiled=True),
        lax.all_gather(norm2_shift, "fsdp", axis=0, tiled=True),
        lax.all_gather(router_weight, "fsdp", axis=0, tiled=True),
    )
    expert_back = (
        lax.all_gather(expert_in, "fsdp", axis=1, tiled=True),
        lax.all_gather(expert_in_bias, "fsdp", axis=1, tiled=True),
        lax.all_gather(expert_out, "fsdp", axis=1, tiled=True),
        lax.all_gather(expert_out_bias, "fsdp", axis=1, tiled=True),
    )
    (
        gain_one,
        shift_one,
        w_query,
        b_query,
        w_key,
        w_value,
        b_value,
        w_out,
        b_out,
        gain_two,
        shift_two,
        w_router,
    ) = attn_back
    w_in, b_in, w_exit, b_exit = expert_back
    grad_out = cotangent.astype(f32)
    gate_grad = jnp.einsum("tkd,td->tk", picked, grad_out)
    picked_grad = (gates[:, :, None] * grad_out[:, None, :]).astype(bf16)
    exit_grad = (
        jnp.zeros((EXP * CAP, D), bf16)
        .at[flat_cells]
        .set(picked_grad.reshape(-1, D))
        .reshape(EXP, CAP, D)
    )
    b_exit_grad = jnp.sum(exit_grad, 1, dtype=f32)
    activ_grad = jnp.einsum("ecd,efd->ecf", exit_grad, w_exit, preferred_element_type=f32)
    gelu_back = jax.vjp(smooth_gelu, inner)[1]
    inner_grad = gelu_back(activ_grad)[0].astype(bf16)
    b_in_grad = jnp.sum(inner_grad, 1, dtype=f32)
    block_grad = jnp.einsum("ecf,edf->ecd", inner_grad, w_in, preferred_element_type=f32).reshape(
        EXP * CAP, D
    )
    hidden_b_grad = jnp.sum(block_grad[cell_index], 1)
    chosen_grad = gates * (gate_grad - jnp.sum(gates * gate_grad, -1, keepdims=True))
    logit_grad = jnp.einsum("tk,tke->te", chosen_grad, one_hot).astype(bf16)
    router_grad = jnp.einsum("td,te->de", hidden_b, logit_grad, preferred_element_type=f32)
    hidden_b_grad = hidden_b_grad + jnp.einsum(
        "te,de->td", logit_grad, w_router, preferred_element_type=f32
    )
    resid_part, gain_two_grad, shift_two_grad = norm_back(
        hidden_b_grad, unit_b, rstd_b, gain_two.astype(f32)
    )
    resid_grad = grad_out + resid_part
    branch_grad = resid_grad.astype(bf16)
    b_out_grad = jnp.sum(branch_grad, 0, dtype=f32)
    w_out_grad = jnp.einsum("td,te->de", attended, branch_grad, preferred_element_type=f32)
    attended_grad = (
        jnp.einsum("te,de->td", branch_grad, w_out, preferred_element_type=f32)
        .astype(bf16)
        .reshape(heads_shape)
    )
    scores_again = jnp.einsum("ishd,ithd->ihst", query_h, key_h, preferred_element_type=f32) * SCALE
    probs_again = jnp.exp(scores_again - log_total)
    value_grad = (
        jnp.einsum(
            "ihst,ishd->ithd", probs_again.astype(bf16), attended_grad, preferred_element_type=f32
        )
        .astype(bf16)
        .reshape(tok_rows, D)
    )
    prob_grad = jnp.einsum("ishd,ithd->ihst", attended_grad, value_h, preferred_element_type=f32)
    score_grad = (
        probs_again * (prob_grad - jnp.sum(probs_again * prob_grad, -1, keepdims=True))
    ).astype(bf16)
    query_grad = (
        (jnp.einsum("ihst,ithd->ishd", score_grad, key_h, preferred_element_type=f32) * SCALE)
        .astype(bf16)
        .reshape(tok_rows, D)
    )
    key_grad = (
        (jnp.einsum("ihst,ishd->ithd", score_grad, query_h, preferred_element_type=f32) * SCALE)
        .astype(bf16)
        .reshape(tok_rows, D)
    )
    b_query_grad = jnp.sum(query_grad, 0, dtype=f32)
    b_value_grad = jnp.sum(value_grad, 0, dtype=f32)
    w_query_grad = jnp.einsum("td,te->de", hidden_a, query_grad, preferred_element_type=f32)
    w_key_grad = jnp.einsum("td,te->de", hidden_a, key_grad, preferred_element_type=f32)
    w_value_grad = jnp.einsum("td,te->de", hidden_a, value_grad, preferred_element_type=f32)
    hidden_a_grad = jnp.einsum("te,de->td", query_grad, w_query, preferred_element_type=f32)
    hidden_a_grad = hidden_a_grad + jnp.einsum(
        "te,de->td", key_grad, w_key, preferred_element_type=f32
    )
    hidden_a_grad = hidden_a_grad + jnp.einsum(
        "te,de->td", value_grad, w_value, preferred_element_type=f32
    )
    input_part, gain_one_grad, shift_one_grad = norm_back(
        hidden_a_grad, unit_a, rstd_a, gain_one.astype(f32)
    )
    tokens_grad = resid_grad + input_part
    attn_sums = (
        lax.psum_scatter(gain_one_grad, "fsdp", scatter_dimension=0, tiled=True),
        lax.psum_scatter(shift_one_grad, "fsdp", scatter_dimension=0, tiled=True),
        lax.psum_scatter(w_query_grad, "fsdp", scatter_dimension=0, tiled=True),
        lax.psum_scatter(b_query_grad, "fsdp", scatter_dimension=0, tiled=True),
        lax.psum_scatter(w_key_grad, "fsdp", scatter_dimension=0, tiled=True),
        lax.psum_scatter(w_value_grad, "fsdp", scatter_dimension=0, tiled=True),
        lax.psum_scatter(b_value_grad, "fsdp", scatter_dimension=0, tiled=True),
        lax.psum_scatter(w_out_grad, "fsdp", scatter_dimension=0, tiled=True),
        lax.psum_scatter(b_out_grad, "fsdp", scatter_dimension=0, tiled=True),
        lax.psum_scatter(gain_two_grad, "fsdp", scatter_dimension=0, tiled=True),
        lax.psum_scatter(shift_two_grad, "fsdp", scatter_dimension=0, tiled=True),
        lax.psum_scatter(router_grad, "fsdp", scatter_dimension=0, tiled=True),
        lax.psum_scatter(b_in_grad.T, "fsdp", scatter_dimension=0, tiled=True),
        lax.psum_scatter(b_exit_grad.T, "fsdp", scatter_dimension=0, tiled=True),
    )
    w_in_sum = lax.psum_scatter(
        jnp.einsum("ecd,ecf->def", blocks, inner_grad, preferred_element_type=f32),
        "fsdp",
        scatter_dimension=0,
        tiled=True,
    )
    w_exit_sum = lax.psum_scatter(
        jnp.einsum("ecf,ecd->fed", activ, exit_grad, preferred_element_type=f32),
        "fsdp",
        scatter_dimension=0,
        tiled=True,
    )
    attn_part = tuple(attn_sums[:12])
    b_in_sum = attn_sums[12].T
    b_exit_sum = attn_sums[13].T
    return (
        (mixed_out, tokens_grad)
        + attn_part
        + (
            jnp.transpose(w_in_sum, (1, 0, 2)),
            b_in_sum,
            jnp.transpose(w_exit_sum, (1, 0, 2)),
            b_exit_sum,
        )
    )


def solution(mesh):
    in_specs = (
        P("fsdp", None),
        P("fsdp", None),
        P("fsdp", None),
        P("fsdp", None),
        P("fsdp"),
        P("fsdp"),
        P("fsdp", None),
        P("fsdp"),
        P("fsdp", None),
        P("fsdp", None),
        P("fsdp"),
        P("fsdp", None),
        P("fsdp"),
        P("fsdp"),
        P("fsdp"),
        P("fsdp", None),
        P(None, "fsdp", None),
        P(None, "fsdp"),
        P(None, "fsdp", None),
        P(None, "fsdp"),
    )
    out_specs = (
        P("fsdp", None),
        P("fsdp", None),
        P("fsdp"),
        P("fsdp"),
        P("fsdp", None),
        P("fsdp"),
        P("fsdp", None),
        P("fsdp", None),
        P("fsdp"),
        P("fsdp", None),
        P("fsdp"),
        P("fsdp"),
        P("fsdp"),
        P("fsdp", None),
        P(None, "fsdp", None),
        P(None, "fsdp"),
        P(None, "fsdp", None),
        P(None, "fsdp"),
    )
    return jax.shard_map(
        per_device, mesh=mesh, in_specs=in_specs, out_specs=out_specs, check_vma=False
    )
```

profile of v0, /device:TPU:0, one launch (start us, length us, event | category | flops | bytes accessed | tf_op | source)
XLA Modules:
  0.0 2180.4 jit_solution(1013712668404914216)
XLA Ops:
  17.1 42.2 %all-reduce.19 = (bf16[768]{0:T(1024)(128)(2,1)S(1)}, bf16[768]{0:T(1024)(128)(2,1)S(1)}, bf16[768]{0:T(1024)(128)(2,1)S(1)}, bf16[768]{0:T(1024)(128)(2,1)S(1)}...) all-reduce(bf16[768]{0:T(1024)(128)(2,1)S(1)} %dynamic-update-slice, ...), channel_id=1, replica_groups=mesh['fsdp'=32] {'fsdp'}, use_global_device_ids=true, to_apply=%add.2 | all-reduce | flops 5376 | bytes 21504
  59.5 40.6 %all-gather = bf16[32,24,4]{1,2,0:T(4,128)(2,1)S(1)} all-gather(bf16[1,24,4]{1,2,0:T(4,128)(2,1)} %bitcast.138), channel_id=1, replica_groups=mesh['fsdp'=32] {'fsdp'}, dimensions={0}, use_global_device_ids=true | all-gather | bytes 6336 | tf_op jit(solution)/shard_map/all_gather | solution.py:82
  100.2 36.7 %all-gather.1 = bf16[32,96,4]{1,2,0:T(4,128)(2,1)S(1)} all-gather(bf16[1,96,4]{1,2,0:T(4,128)(2,1)S(1)} %bitcast.139), channel_id=1, replica_groups=mesh['fsdp'=32] {'fsdp'}, dimensions={0}, use_global_device_ids=true | all-gather | bytes 25344 | tf_op jit(solution)/shard_map/all_gather | solution.py:86
  137.0 38.0 %all-gather.2 = bf16[32,24,4]{1,2,0:T(4,128)(2,1)S(1)} all-gather(bf16[1,24,4]{1,2,0:T(4,128)(2,1)S(1)} %bitcast.140), channel_id=1, replica_groups=mesh['fsdp'=32] {'fsdp'}, dimensions={0}, use_global_device_ids=true | all-gather | bytes 6336 | tf_op jit(solution)/shard_map/all_gather | solution.py:88
  206.9 28.6 %all-gather.16.cloned.1.call-done = bf16[768,768]{1,0:T(8,128)(2,1)} async-done(((bf16[24,768]{1,0:T(8,128)(2,1)}), bf16[768,768]{1,0:T(8,128)(2,1)}) %all-gather.16.cloned.1.call-update) | async-done | bytes 1179664 | tf_op jit(solution)/shard_map/all_gather | solution.py:78
  241.2 7.6 scatter_custom_fusion
  252.4 109.5 %all-gather.18.cloned.1.call-done = bf16[4,768,3072]{2,1,0:T(8,128)(2,1)} async-done(((bf16[4,24,3072]{2,1,0:T(8,128)(2,1)}), bf16[4,768,3072]{2,1,0:T(8,128)(2,1)}) %all-gather.18.cloned.1.call-update) | async-done | bytes 18874384 | tf_op jit(solution)/shard_map/all_gather | solution.py:85
  361.9 14.1 fusion.79
  376.0 111.5 %all-gather.20.cloned.1.call-done = bf16[4,3072,768]{2,1,0:T(8,128)(2,1)} async-done(((bf16[4,96,768]{2,1,0:T(8,128)(2,1)}), bf16[4,3072,768]{2,1,0:T(8,128)(2,1)}) %all-gather.20.cloned.1.call-update) | async-done | bytes 18874384 | tf_op jit(solution)/shard_map/all_gather | solution.py:87
  487.5 16.2 convolution_add_fusion
  515.6 9.0 scatter_custom_fusion.1
  526.4 19.6 convert_reduce_fusion
  547.8 18.3 convolution_bitcast_fusion
  566.1 43.2 %copy.139 = f32[3072,4,768]{2,1,0:T(4,128)} copy(f32[3072,4,768]{0,2,1:T(8,128)} %convolution_bitcast_fusion) | data formatting | bytes 75497472 | tf_op jit(solution)/shard_map/ecf,ecd->fed/transpose | solution.py:292
  610.7 17.7 convolution_bitcast_fusion.1
  628.4 44.5 %copy.138 = f32[768,4,3072]{2,1,0:T(4,128)} copy(f32[768,4,3072]{0,2,1:T(8,128)} %convolution_bitcast_fusion.1) | data formatting | bytes 75497472 | tf_op jit(solution)/shard_map/ecd,ecf->def/transpose | solution.py:286
  673.0 13.0 fusion.80
  755.2 41.4 %all-reduce.18 = (f32[768]{0:T(1024)S(1)}, f32[768]{0:T(1024)S(1)}, f32[768]{0:T(1024)S(1)}, f32[768]{0:T(1024)S(1)}, f32[768]{0:T(1024)S(1)}, /*index=5*/f32[76...) all-reduce(f32[768]{0:T(1024)S(1)} %get-tuple-element.92, ...), channel_id=2, replica_groups=mesh['fsdp'=32] {'fsdp'}, use_global_device_ids=true, to_apply=%region_18.0.clone | all-reduce | flops 11520 | bytes 92160
  806.2 392.9 %all-reduce.25.cloned.1.call-done = f32[3072,4,768]{2,1,0:T(4,128)} async-done(((f32[3072,4,768]{2,1,0:T(4,128)}), f32[3072,4,768]{2,1,0:T(4,128)}) %all-reduce.25.cloned.1.call-update) | async-done | bytes 37748752
  1201.8 553.5 %all-reduce.23.cloned.1.call-done = f32[768,4,3072]{2,1,0:T(4,128)} async-done(((f32[768,4,3072]{2,1,0:T(4,128)}), f32[768,4,3072]{2,1,0:T(4,128)}) %all-reduce.23.cloned.1.call-update) | async-done | bytes 37748752
  1758.4 101.7 %reduce-scatter.16.cloned.1.call-done = f32[24,768]{1,0:T(8,128)} async-done(((f32[768,768]{1,0:T(8,128)}), f32[24,768]{1,0:T(8,128)}) %reduce-scatter.16.cloned.1.call-update) | async-done | bytes 73744 | tf_op jit(solution)/shard_map/reduce_scatter | solution.py:277
  1860.1 104.7 %reduce-scatter.14.cloned.1.call-done = f32[24,768]{1,0:T(8,128)} async-done(((f32[768,768]{1,0:T(8,128)}), f32[24,768]{1,0:T(8,128)}) %reduce-scatter.14.cloned.1.call-update) | async-done | bytes 73744 | tf_op jit(solution)/shard_map/reduce_scatter | solution.py:275
  1964.8 103.8 %reduce-scatter.12.cloned.1.call-done = f32[24,768]{1,0:T(8,128)} async-done(((f32[768,768]{1,0:T(8,128)}), f32[24,768]{1,0:T(8,128)}) %reduce-scatter.12.cloned.1.call-update) | async-done | bytes 73744 | tf_op jit(solution)/shard_map/reduce_scatter | solution.py:274
  2068.7 104.7 %reduce-scatter.10.cloned.1.call-done = f32[24,768]{1,0:T(8,128)} async-done(((f32[768,768]{1,0:T(8,128)}), f32[24,768]{1,0:T(8,128)}) %reduce-scatter.10.cloned.1.call-update) | async-done | bytes 73744 | tf_op jit(solution)/shard_map/reduce_scatter | solution.py:272
  (308 shorter events, 151.4 us)
Async XLA Ops:
  7.2 93.0 %copy-start.71 = (bf16[4,96]{1,0:T(4,128)(2,1)S(1)}, bf16[4,96]{1,0:T(4,128)(2,1)}, u32[]{:S(2)}) copy-start(bf16[4,96]{1,0:T(4,128)(2,1)} %param.37) | copy-start | bytes 2308
  7.2 129.8 %copy-start.72 = (bf16[4,24]{1,0:T(4,128)(2,1)S(1)}, bf16[4,24]{1,0:T(4,128)(2,1)}, u32[]{:S(2)}) copy-start(bf16[4,24]{1,0:T(4,128)(2,1)} %param.39) | copy-start | bytes 580
  7.2 168.1 %copy-start.58 = (s32[394,2]{0,1:T(2,128)S(1)}, s32[394,2]{0,1:T(2,128)}, u32[]{:S(2)}) copy-start(s32[394,2]{0,1:T(2,128)} %param.22) | copy-start | bytes 9460
  7.2 168.3 %copy-start.70 = (s32[394,2]{0,1:T(2,128)S(1)}, s32[394,2]{0,1:T(2,128)}, u32[]{:S(2)}) copy-start(s32[394,2]{0,1:T(2,128)} %param.23) | copy-start | bytes 9460
  7.2 175.4 %all-gather.14.cloned.1.call-start = ((), (), s32[]{:S(2)}) async-start(), calls=%async_computation.7 | async-start | bytes 1216512 | tf_op jit(solution)/shard_map/all_gather | solution.py:75
  8.0 179.6 %all-gather.10.cloned.1.call-start = ((), (), s32[]{:S(2)}) async-start(), calls=%async_computation.5 | async-start | bytes 1216512 | tf_op jit(solution)/shard_map/all_gather | solution.py:76
  8.7 186.2 %all-gather.12.cloned.1.call-start = ((), (), s32[]{:S(2)}) async-start(), calls=%async_computation.6 | async-start | bytes 1216512 | tf_op jit(solution)/shard_map/all_gather | solution.py:73
  9.4 226.0 %all-gather.16.cloned.1.call-start = ((), (), s32[]{:S(2)}) async-start(), calls=%async_computation.8 | async-start | bytes 1216512 | tf_op jit(solution)/shard_map/all_gather | solution.py:78
  10.0 166.1 %copy-start.25 = (bf16[394,768]{1,0:T(8,128)(2,1)S(1)}, bf16[394,768]{1,0:T(8,128)(2,1)}, u32[]{:S(2)}) copy-start(bf16[394,768]{1,0:T(8,128)(2,1)} %param.21) | copy-start | bytes 1815556
  10.0 351.8 %all-gather.18.cloned.1.call-start = ((), (), s32[]{:S(2)}) async-start(), calls=%async_computation.9 | async-start | bytes 19464192 | tf_op jit(solution)/shard_map/all_gather | solution.py:85
  10.6 476.9 %all-gather.20.cloned.1.call-start = ((), (), s32[]{:S(2)}) async-start(), calls=%async_computation.10 | async-start | bytes 19464192 | tf_op jit(solution)/shard_map/all_gather | solution.py:87
  11.2 793.6 %reduce-scatter.18.cloned.1.call-start = ((), (), s32[]{:S(2)}) async-start(), calls=%async_computation.15 | async-start | bytes 1622016
  59.4 135.6 %copy-start.53 = (f32[768]{0:T(1024)}, f32[768]{0:T(1024)S(1)}, u32[]{:S(2)}) copy-start(f32[768]{0:T(1024)S(1)} %convert_element_type.124) | copy-start | bytes 9220
  59.4 135.6 %copy-start.67 = (f32[768]{0:T(1024)}, f32[768]{0:T(1024)S(1)}, u32[]{:S(2)}) copy-start(f32[768]{0:T(1024)S(1)} %convert_element_type.125) | copy-start | bytes 9220
  59.4 178.5 %copy-start.40 = (f32[768]{0:T(1024)}, f32[768]{0:T(1024)S(1)}, u32[]{:S(2)}) copy-start(f32[768]{0:T(1024)S(1)} %convert_element_type.136) | copy-start | bytes 9220
  100.2 138.0 %copy-start.42 = (bf16[768,4]{0,1:T(4,128)(2,1)}, bf16[768,4]{0,1:T(4,128)(2,1)S(1)}, u32[]{:S(2)}) copy-start(bf16[768,4]{0,1:T(4,128)(2,1)S(1)} %reshape.243) | copy-start | bytes 18436
  175.5 75.2 %copy-start.36 = (s32[394,2]{1,0:T(8,128)}, s32[394,2]{1,0:T(8,128)S(1)}, u32[]{:S(2)}) copy-start(s32[394,2]{1,0:T(8,128)S(1)} %copy.120) | copy-start | bytes 9460
  250.7 111.2 %copy-start.5 = (bf16[4,246,768]{2,1,0:T(8,128)(2,1)}, bf16[4,246,768]{2,1,0:T(8,128)(2,1)S(1)}, u32[]{:S(2)}) copy-start(bf16[4,246,768]{2,1,0:T(8,128)(2,1)S(1)} %reshape.184) | copy-start | bytes 4534276
  547.7 651.5 %all-reduce.25.cloned.1.call-start = ((), (), s32[]{:S(2)}) async-start(), calls=%async_computation.17 | async-start | bytes 75497472
  609.4 1145.9 %all-reduce.23.cloned.1.call-start = ((), (), s32[]{:S(2)}) async-start(), calls=%async_computation.16 | async-start | bytes 75497472
  672.9 1187.2 %reduce-scatter.16.cloned.1.call-start = ((), (), s32[]{:S(2)}) async-start(), calls=%async_computation.14 | async-start | bytes 2433024 | tf_op jit(solution)/shard_map/reduce_scatter | solution.py:277
  709.4 1255.4 %reduce-scatter.14.cloned.1.call-start = ((), (), s32[]{:S(2)}) async-start(), calls=%async_computation.13 | async-start | bytes 2433024 | tf_op jit(solution)/shard_map/reduce_scatter | solution.py:275
  722.6 1346.0 %reduce-scatter.12.cloned.1.call-start = ((), (), s32[]{:S(2)}) async-start(), calls=%async_computation.12 | async-start | bytes 2433024 | tf_op jit(solution)/shard_map/reduce_scatter | solution.py:274
  740.7 1432.6 %reduce-scatter.10.cloned.1.call-start = ((), (), s32[]{:S(2)}) async-start(), calls=%async_computation.11 | async-start | bytes 2433024 | tf_op jit(solution)/shard_map/reduce_scatter | solution.py:272
  (63 other events, 247.4 us)
Sparse Core Ops, SparseCore 0:
  11.0 57.0 all-gather.13
  71.0 52.8 all-gather.9
  126.8 52.9 all-gather.11
  182.5 52.9 all-gather.15
  238.3 123.5 all-gather.17
  364.7 122.7 all-gather.19
  547.8 95.1 reduce-scatter.17
  649.4 549.7 all-reduce.24
  1205.6 549.6 all-reduce.22
  1761.0 99.0 reduce-scatter.15
  1866.8 97.9 reduce-scatter.13
  1970.5 98.0 reduce-scatter.11
  2075.4 97.9 reduce-scatter.9
where the time goes:
time: 2190 us; the launch traced here: 2180 us
  waiting for transfers between devices  1610 us (74%)
  blocking collectives  199 us (9%)
  local copies, waits for them, and re-layouts  175 us (8%)
  matrix products  148 us (7%)
  other arithmetic  27 us (1%)
    unnamed x16, waiting for transfers between devices  950 us
    all_gather x1, waiting for transfers between devices, per_device(): lax.all_gather(expert_out, 'fsdp', axis=1, tiled=True)  112 us
    all_gather x1, waiting for transfers between devices, per_device(): lax.all_gather(expert_in, 'fsdp', axis=1, tiled=True)  109 us
    reduce_scatter x1, waiting for transfers between devices, per_device(): lax.psum_scatter(w_value_grad, 'fsdp', scatter_dimension=0, tiled=True)  105 us
    reduce_scatter x1, waiting for transfers between devices, per_device(): lax.psum_scatter(w_query_grad, 'fsdp', scatter_dimension=0, tiled=True)  105 us
    reduce_scatter x1, waiting for transfers between devices, per_device(): lax.psum_scatter(w_key_grad, 'fsdp', scatter_dimension=0, tiled=True)  104 us
    reduce_scatter x1, waiting for transfers between devices, per_device(): lax.psum_scatter(w_out_grad, 'fsdp', scatter_dimension=0, tiled=True)  102 us
    unnamed x2, blocking collectives  83.7 us
  transfers between devices with their start and end apart: 13, of which 9 were waited for; matrix products, arithmetic and copies ran while one was open for 13% of the time, Pallas kernels for 0%

commit v1 on v0

v1 whole, which is shorter than its diff:
```python
import functools

import jax
import jax.numpy as jnp
from jax import lax
from jax.experimental import pallas as pl
from jax.experimental.pallas import tpu as pltpu
from jax.sharding import PartitionSpec as P

D = 768
HEADS = 12
HEAD_DIM = 64
EXP = 4
SEQ = 197
CAP = 246
CELLS = 256


EPSILON = 1e-05
SCALE = 0.125
F32 = jnp.float32
BF16 = jnp.bfloat16
AXIS = "fsdp"

GROUP_BITS = (0, 3)


def group_mask(k):
    return (k & 1) << GROUP_BITS[0] | (k >> 1) << GROUP_BITS[1]


def norm_rows(values, gain, shift):
    mean_row = jnp.mean(values, -1, keepdims=True)
    centred = values - mean_row
    rstd_row = lax.rsqrt(jnp.mean(centred * centred, -1, keepdims=True) + EPSILON)
    unit_rows = centred * rstd_row
    return (unit_rows * gain + shift, unit_rows, rstd_row)


def norm_back(grad_in, unit_rows, rstd_row, gain):
    scaled = grad_in * gain
    input_grad = rstd_row * (
        scaled
        - jnp.mean(scaled, -1, keepdims=True)
        - unit_rows * jnp.mean(scaled * unit_rows, -1, keepdims=True)
    )
    return (input_grad, jnp.sum(grad_in * unit_rows, 0), jnp.sum(grad_in, 0))


def smooth_gelu(inner):
    return 0.5 * inner * (1.0 + jnp.tanh(0.7978845608 * (inner + 0.044715 * inner * inner * inner)))


def swap(x, n, mask):
    return lax.ppermute(x, AXIS, [(i, i ^ mask) for i in range(n)])


def bit_of(me, bit):
    return (me >> bit) & 1


def gather_all(x, n, me, order):
    width = n.bit_length() - 1
    x = x.reshape((1,) * width + x.shape)
    for bit in order:
        axis = width - 1 - bit
        other = swap(x, n, 1 << bit)
        high = bit_of(me, bit) == 1
        x = jnp.concatenate([jnp.where(high, other, x), jnp.where(high, x, other)], axis)
    return x.reshape((n,) + x.shape[width:])


def halve(x, n, me, bit, axis):
    mine = bit_of(me, bit)
    send = lax.dynamic_index_in_dim(x, 1 - mine, axis, keepdims=True)
    keep = lax.dynamic_index_in_dim(x, mine, axis, keepdims=True)
    other = swap(send, n, 1 << bit)
    return (keep.astype(F32) + other.astype(F32)).astype(BF16)


def scatter_sum(x, n, me, order):
    width = n.bit_length() - 1
    tail = x.shape[1:]
    x = x.reshape((2,) * width + tail)
    for bit in order:
        x = halve(x, n, me, bit, width - 1 - bit)
    return x.reshape(tail)


def place_kernel(masks, pair_rows, me_ref, *refs):
    pieces, out, sems = refs[: len(masks)], refs[len(masks)], refs[len(masks) + 1]
    copies = []
    for j, mask in enumerate(masks):
        for z in range(2):
            pair = (me_ref[0] ^ (mask | z << GROUP_BITS[1])) >> 1
            copies.append(
                pltpu.make_async_copy(
                    pieces[j].at[z],
                    out.at[pl.ds(pl.multiple_of(pair * pair_rows, pair_rows), pair_rows)],
                    sems.at[2 * j + z],
                )
            )
    for copy in copies:
        copy.start()
    for copy in copies:
        copy.wait()


def place(pieces, n, me):
    masks = sorted(pieces)
    _, pair_rows, columns = pieces[0].shape
    rows = pair_rows * (n // 2)
    if pair_rows % 16 == 0:
        return pl.pallas_call(
            functools.partial(place_kernel, masks, pair_rows),
            out_shape=jax.ShapeDtypeStruct((rows, columns), BF16),
            in_specs=[pl.BlockSpec(memory_space=pltpu.SMEM)]
            + [pl.BlockSpec(memory_space=pl.ANY)] * len(masks),
            out_specs=pl.BlockSpec(memory_space=pl.ANY),
            scratch_shapes=[pltpu.SemaphoreType.DMA((2 * len(masks),))],
        )(me.reshape(1).astype(jnp.int32), *[pieces[mask] for mask in masks])
    by_mask = [None] * (n // 2)
    for mask in masks:
        for z in range(2):
            by_mask[(mask | z << GROUP_BITS[1]) >> 1] = pieces[mask][z]
    order = jnp.arange(n // 2, dtype=jnp.int32) ^ (me >> 1)
    return jnp.take(jnp.stack(by_mask), order, axis=0).reshape(rows, columns)


def expert_gather(shard, n, me, expert, order):
    own = [
        lax.dynamic_index_in_dim(shard, expert ^ k, 0, keepdims=False) for k in range(EXP)
    ]
    got = [own[0]] + [swap(own[k], n, group_mask(k)) for k in range(1, EXP)]
    high = bit_of(me, GROUP_BITS[0]) == 1
    rows, columns = shard.shape[1:]
    block = jnp.stack(
        [
            jnp.stack([jnp.where(high, odd, even), jnp.where(high, even, odd)])
            for even, odd in ((got[0], got[1]), (got[2], got[3]))
        ]
    ).reshape(2, 2 * rows, columns)
    pieces = {0: block}
    for bit in order:
        for mask in list(pieces):
            pieces[mask | 1 << bit] = swap(pieces[mask], n, 1 << bit)
    return place(pieces, n, me)


def expert_scatter(grad, n, me, expert, order):
    width = n.bit_length() - 1
    rows, columns = grad.shape[0] // n, grad.shape[1]
    x = grad.reshape((2,) * width + (rows, columns))
    for bit in order:
        x = halve(x, n, me, bit, width - 1 - bit)
    x = x.reshape(2, 2, rows, columns)
    own_z, own_c = bit_of(me, GROUP_BITS[1]), bit_of(me, GROUP_BITS[0])
    got = []
    for k in range(EXP):
        part = lax.dynamic_slice(
            x, (own_z ^ (k >> 1), own_c ^ (k & 1), 0, 0), (1, 1, rows, columns)
        ).reshape(rows, columns)
        got.append(part if k == 0 else swap(part, n, group_mask(k)))
    places = jnp.arange(EXP, dtype=jnp.int32) ^ expert
    return jnp.stack(
        [
            lax.select_n(places[i], *got).astype(F32)
            for i in range(EXP)
        ]
    )


def per_device(
    n,
    tokens,
    cotangent,
    expert_ids,
    slots,
    norm1_gain,
    norm1_shift,
    query_weight,
    query_bias,
    key_weight,
    value_weight,
    value_bias,
    out_weight,
    out_bias,
    norm2_gain,
    norm2_shift,
    router_weight,
    expert_in,
    expert_in_bias,
    expert_out,
    expert_out_bias,
):
    me = lax.axis_index(AXIS)
    width = n.bit_length() - 1
    expert = bit_of(me, GROUP_BITS[0]) | bit_of(me, GROUP_BITS[1]) << 1
    far_bits = [b for b in range(width) if b not in GROUP_BITS and b > 2][::-1]
    x_first = far_bits + [1, 2]
    y_first = far_bits + [2, 1]
    rows = query_weight.shape[0]
    ff_rows = expert_out.shape[1]
    ff = ff_rows * n
    tok_rows = tokens.shape[0]
    images = tok_rows // SEQ
    heads_shape = (images, SEQ, HEADS, HEAD_DIM)

    vectors = jnp.stack(
        [norm1_gain, norm1_shift, query_bias, value_bias, out_bias, norm2_gain, norm2_shift]
    )
    small = jnp.concatenate(
        [vectors, router_weight.T, expert_out_bias], 0
    ).reshape(-1)
    small = jnp.concatenate([small, expert_in_bias.reshape(-1)])
    n_small = small.shape[0]
    small = jnp.pad(small, (0, D - n_small)).reshape(1, D)
    pack_a = jnp.concatenate([query_weight, key_weight], 0)
    pack_b = jnp.concatenate([value_weight, out_weight, small], 0)
    full_a = gather_all(pack_a, n, me, far_bits + [3, 1, 2, 0])
    full_b = gather_all(pack_b, n, me, far_bits + [3, 2, 1, 0])
    w_query = full_a[:, :rows].reshape(D, D)
    w_key = full_a[:, rows:].reshape(D, D)
    w_value = full_b[:, :rows].reshape(D, D)
    w_out = full_b[:, rows : 2 * rows].reshape(D, D)
    small_full = full_b[:, 2 * rows]
    vec = small_full[:, : 15 * rows].reshape(n, 15, rows).transpose(1, 0, 2).reshape(15, D)
    gain_one, shift_one, b_query, b_value, b_out, gain_two, shift_two = [
        vec[i].astype(F32) for i in range(7)
    ]
    w_router_t = vec[7:11]
    b_exit = lax.dynamic_index_in_dim(vec[11:15], expert, 0, keepdims=True).astype(F32)
    b_in_all = small_full[:, 15 * rows : n_small].reshape(n, EXP, ff_rows)
    b_in = lax.dynamic_index_in_dim(b_in_all, expert, 1, keepdims=False).reshape(1, ff).astype(F32)

    w_in = expert_gather(expert_in, n, me, expert, x_first)
    w_exit = expert_gather(expert_out, n, me, expert, y_first)

    cell_index = (expert_ids ^ expert) * CELLS + slots
    cell_ids = jnp.arange(EXP * CELLS, dtype=jnp.int32)
    hit_rows = [
        (cell_index[:, k][None, :] == cell_ids[:, None]) for k in range(2)
    ]
    spread = (hit_rows[0] | hit_rows[1]).astype(BF16)
    cot_cells = jnp.dot(spread, cotangent, preferred_element_type=F32).astype(BF16)

    def to_experts(cells):
        parts = cells.reshape((EXP, CELLS) + cells.shape[1:])
        return jnp.concatenate(
            [parts[0]] + [swap(parts[k], n, group_mask(k)) for k in range(1, EXP)], 0
        )

    cot_blocks = to_experts(cot_cells)

    inputs = tokens.astype(F32)
    normed_a, unit_a, rstd_a = norm_rows(inputs, gain_one, shift_one)
    hidden_a = normed_a.astype(BF16)
    query = (jnp.dot(hidden_a, w_query, preferred_element_type=F32) + b_query).astype(BF16)
    keys_all = jnp.dot(hidden_a, w_key, preferred_element_type=F32).astype(BF16)
    values_all = (jnp.dot(hidden_a, w_value, preferred_element_type=F32) + b_value).astype(BF16)
    query_h = query.reshape(heads_shape)
    key_h = keys_all.reshape(heads_shape)
    value_h = values_all.reshape(heads_shape)
    scores = jnp.einsum("ishd,ithd->ihst", query_h, key_h, preferred_element_type=F32) * SCALE
    row_max = jnp.max(scores, -1, keepdims=True)
    raised = jnp.exp(scores - row_max)
    row_total = jnp.sum(raised, -1, keepdims=True)
    probs = raised / row_total
    log_total = row_max + jnp.log(row_total)
    mixed_h = jnp.einsum("ihst,ithd->ishd", probs.astype(BF16), value_h, preferred_element_type=F32)
    attended = mixed_h.astype(BF16).reshape(tok_rows, D)
    branch_a = jnp.dot(attended, w_out, preferred_element_type=F32) + b_out
    resid = inputs + branch_a
    normed_b, unit_b, rstd_b = norm_rows(resid, gain_two, shift_two)
    hidden_b = normed_b.astype(BF16)

    logits = lax.dot_general(
        hidden_b, w_router_t, (((1,), (1,)), ((), ())), preferred_element_type=F32
    )
    one_hot = expert_ids[:, :, None] == jnp.arange(EXP, dtype=jnp.int32)[None, None, :]
    chosen = jnp.sum(jnp.where(one_hot, logits[:, None, :], 0.0), -1)
    chosen_max = jnp.max(chosen, -1, keepdims=True)
    chosen_exp = jnp.exp(chosen - chosen_max)
    gates = chosen_exp / jnp.sum(chosen_exp, -1, keepdims=True)
    blocks = to_experts(jnp.dot(spread, hidden_b, preferred_element_type=F32).astype(BF16))
    gate_cells = jnp.sum(
        jnp.where(hit_rows[0], gates[:, 0][None, :], 0.0)
        + jnp.where(hit_rows[1], gates[:, 1][None, :], 0.0),
        1,
    )
    gate_blocks = to_experts(gate_cells.reshape(EXP * CELLS // 128, 128).reshape(EXP * CELLS))
    inner = jnp.dot(blocks, w_in, preferred_element_type=F32) + b_in
    activ = smooth_gelu(inner).astype(BF16)
    expert_y = (jnp.dot(activ, w_exit, preferred_element_type=F32) + b_exit).astype(BF16)

    exit_grad = (gate_blocks[:, None] * cot_blocks.astype(F32)).astype(BF16)
    b_exit_grad = jnp.sum(exit_grad, 0, dtype=F32)
    activ_grad = lax.dot_general(
        exit_grad, w_exit, (((1,), (1,)), ((), ())), preferred_element_type=F32
    )
    inner_grad = jax.vjp(smooth_gelu, inner)[1](activ_grad)[0].astype(BF16)
    b_in_grad = jnp.sum(inner_grad, 0, dtype=F32)
    block_grad = lax.dot_general(
        inner_grad, w_in, (((1,), (1,)), ((), ())), preferred_element_type=F32
    ).astype(BF16)
    w_exit_grad = lax.dot_general(
        activ, exit_grad, (((0,), (0,)), ((), ())), preferred_element_type=F32
    ).astype(BF16)
    w_in_grad = lax.dot_general(
        blocks, inner_grad, (((0,), (0,)), ((), ())), preferred_element_type=F32
    ).astype(BF16)
    y_cells = to_experts(expert_y)
    grad_cells = to_experts(block_grad)
    w_in_sum = expert_scatter(w_in_grad, n, me, expert, x_first[::-1])
    w_exit_sum = expert_scatter(w_exit_grad, n, me, expert, y_first[::-1])

    grad_out = cotangent.astype(F32)
    picked = [
        lax.dot_general(
            hit_rows[k].astype(BF16), y_cells, (((0,), (0,)), ((), ())), preferred_element_type=F32
        )
        for k in range(2)
    ]
    mixed_out = (resid + (gates[:, :1] * picked[0] + gates[:, 1:] * picked[1])).astype(BF16)
    gate_grad = jnp.stack([jnp.sum(picked[k] * grad_out, -1) for k in range(2)], -1)
    hidden_b_grad = lax.dot_general(
        spread, grad_cells, (((0,), (0,)), ((), ())), preferred_element_type=F32
    )
    chosen_grad = gates * (gate_grad - jnp.sum(gates * gate_grad, -1, keepdims=True))
    logit_grad = jnp.sum(jnp.where(one_hot, chosen_grad[:, :, None], 0.0), 1).astype(BF16)
    router_grad_t = lax.dot_general(
        logit_grad, hidden_b, (((0,), (0,)), ((), ())), preferred_element_type=F32
    )
    hidden_b_grad = hidden_b_grad + jnp.dot(logit_grad, w_router_t, preferred_element_type=F32)
    resid_part, gain_two_grad, shift_two_grad = norm_back(hidden_b_grad, unit_b, rstd_b, gain_two)
    resid_grad = grad_out + resid_part
    branch_grad = resid_grad.astype(BF16)
    b_out_grad = jnp.sum(branch_grad, 0, dtype=F32)
    w_out_grad = jnp.einsum("td,te->de", attended, branch_grad, preferred_element_type=F32)
    attended_grad = (
        jnp.einsum("te,de->td", branch_grad, w_out, preferred_element_type=F32)
        .astype(BF16)
        .reshape(heads_shape)
    )
    scores_again = jnp.einsum("ishd,ithd->ihst", query_h, key_h, preferred_element_type=F32) * SCALE
    probs_again = jnp.exp(scores_again - log_total)
    value_grad = (
        jnp.einsum(
            "ihst,ishd->ithd", probs_again.astype(BF16), attended_grad, preferred_element_type=F32
        )
        .astype(BF16)
        .reshape(tok_rows, D)
    )
    prob_grad = jnp.einsum("ishd,ithd->ihst", attended_grad, value_h, preferred_element_type=F32)
    score_grad = (
        probs_again * (prob_grad - jnp.sum(probs_again * prob_grad, -1, keepdims=True))
    ).astype(BF16)
    query_grad = (
        (jnp.einsum("ihst,ithd->ishd", score_grad, key_h, preferred_element_type=F32) * SCALE)
        .astype(BF16)
        .reshape(tok_rows, D)
    )
    key_grad = (
        (jnp.einsum("ihst,ishd->ithd", score_grad, query_h, preferred_element_type=F32) * SCALE)
        .astype(BF16)
        .reshape(tok_rows, D)
    )
    b_query_grad = jnp.sum(query_grad, 0, dtype=F32)
    b_value_grad = jnp.sum(value_grad, 0, dtype=F32)
    w_query_grad = jnp.einsum("td,te->de", hidden_a, query_grad, preferred_element_type=F32)
    w_key_grad = jnp.einsum("td,te->de", hidden_a, key_grad, preferred_element_type=F32)
    w_value_grad = jnp.einsum("td,te->de", hidden_a, value_grad, preferred_element_type=F32)
    hidden_a_grad = jnp.einsum("te,de->td", query_grad, w_query, preferred_element_type=F32)
    hidden_a_grad = hidden_a_grad + jnp.einsum(
        "te,de->td", key_grad, w_key, preferred_element_type=F32
    )
    hidden_a_grad = hidden_a_grad + jnp.einsum(
        "te,de->td", value_grad, w_value, preferred_element_type=F32
    )
    input_part, gain_one_grad, shift_one_grad = norm_back(hidden_a_grad, unit_a, rstd_a, gain_one)
    tokens_grad = resid_grad + input_part

    own_expert = (jnp.arange(EXP, dtype=jnp.int32) == expert)[:, None]
    vec_grad = jnp.concatenate(
        [
            jnp.stack(
                [
                    gain_one_grad,
                    shift_one_grad,
                    b_query_grad,
                    b_value_grad,
                    b_out_grad,
                    gain_two_grad,
                    shift_two_grad,
                ]
            ),
            router_grad_t,
            jnp.where(own_expert, b_exit_grad[None, :], 0.0),
        ],
        0,
    ).astype(BF16)
    vec_grad = vec_grad.reshape(15, n, rows).transpose(1, 0, 2).reshape(n, 15 * rows)
    in_grad = jnp.where(own_expert, b_in_grad[None, :], 0.0).astype(BF16)
    in_grad = in_grad.reshape(EXP, n, ff_rows).transpose(1, 0, 2).reshape(n, EXP * ff_rows)
    small_grad = jnp.pad(
        jnp.concatenate([vec_grad, in_grad], 1), ((0, 0), (0, D - n_small))
    ).reshape(n, 1, D)

    def by_owner(grad):
        return grad.astype(BF16).reshape(n, rows, D)

    back_bits = far_bits[::-1]
    sum_b = scatter_sum(
        jnp.concatenate([by_owner(w_value_grad), by_owner(w_out_grad), small_grad], 1),
        n,
        me,
        [0, 1, 2, 3] + back_bits,
    ).astype(F32)
    sum_a = scatter_sum(
        jnp.concatenate([by_owner(w_query_grad), by_owner(w_key_grad)], 1),
        n,
        me,
        [0, 2, 1, 3] + back_bits,
    ).astype(F32)
    small_sum = sum_b[2 * rows]
    vec_sum = small_sum[: 15 * rows].reshape(15, rows)
    b_in_sum = small_sum[15 * rows : n_small].reshape(EXP, ff_rows)
    return (
        mixed_out,
        tokens_grad,
        vec_sum[0],
        vec_sum[1],
        sum_a[:rows],
        vec_sum[2],
        sum_a[rows:],
        sum_b[:rows],
        vec_sum[3],
        sum_b[rows : 2 * rows],
        vec_sum[4],
        vec_sum[5],
        vec_sum[6],
        vec_sum[7:11].T,
        w_in_sum,
        b_in_sum,
        w_exit_sum,
        vec_sum[11:15],
    )


def solution(mesh):
    in_specs = (
        P("fsdp", None),
        P("fsdp", None),
        P("fsdp", None),
        P("fsdp", None),
        P("fsdp"),
        P("fsdp"),
        P("fsdp", None),
        P("fsdp"),
        P("fsdp", None),
        P("fsdp", None),
        P("fsdp"),
        P("fsdp", None),
        P("fsdp"),
        P("fsdp"),
        P("fsdp"),
        P("fsdp", None),
        P(None, "fsdp", None),
        P(None, "fsdp"),
        P(None, "fsdp", None),
        P(None, "fsdp"),
    )
    out_specs = (
        P("fsdp", None),
        P("fsdp", None),
        P("fsdp"),
        P("fsdp"),
        P("fsdp", None),
        P("fsdp"),
        P("fsdp", None),
        P("fsdp", None),
        P("fsdp"),
        P("fsdp", None),
        P("fsdp"),
        P("fsdp"),
        P("fsdp"),
        P("fsdp", None),
        P(None, "fsdp", None),
        P(None, "fsdp"),
        P(None, "fsdp", None),
        P(None, "fsdp"),
    )
    return jax.shard_map(
        functools.partial(per_device, mesh.shape["fsdp"]),
        mesh=mesh,
        in_specs=in_specs,
        out_specs=out_specs,
        check_vma=False,
    )
```

time: 2190 us -> 838 us (0.38)
  waiting for transfers between devices: 1610 us -> 240 us
  Pallas kernels: 0 us -> 288 us
  blocking collectives: 199 us -> 0 us
  local copies, waits for them, and re-layouts: 175 us -> 69.3 us
  starting transfers between devices: 1.06 us -> 64.1 us
  matrix products: 148 us -> 118 us
    unnamed x16 -> x0, waiting for transfers between devices: 950 us -> none
    reduce_scatter x4 -> x0, waiting for transfers between devices: 415 us -> none  [the longest x1 105 us: per_device(): lax.psum_scatter(w_value_grad, 'fsdp', scatter_dimension=0, tiled=True)]
    pallas_call x0 -> x2, Pallas kernels: none -> 288 us  [place(): pl.pallas_call(functools.partial(place_kernel, masks, pair_rows), out_sha...]
    all_gather x6 -> x0, waiting for transfers between devices: 250 us -> none  [the longest x1 112 us: per_device(): lax.all_gather(expert_out, 'fsdp', axis=1, tiled=True)]
    ppermute x0 -> x67, waiting for transfers between devices: none -> 240 us  [swap(): return lax.ppermute(x, AXIS, [(i, i ^ mask) for i in range(n)])]
    all_gather x3 -> x0, blocking collectives: 115 us -> none  [the longest x1 40.6 us: per_device(): lax.all_gather(router_weight, 'fsdp', axis=0, tiled=True)]
    transpose x5 -> x1, local copies, waits for them, and re-layouts: 91.1 us -> 0.05 us  [per_device(): vec_grad.reshape(15, n, rows).transpose(1, 0, 2).reshape(n, 15 * rows)]
    unnamed x2 -> x0, blocking collectives: 83.7 us -> none
  transfers between devices with their start and end apart: 13 -> 67, of which waited for: 9 -> 31; matrix products, arithmetic and copies ran while one was open for 13% -> 25% of each run, Pallas kernels for 0% -> 35%
where the time goes in v1:
time: 838 us; the launch traced here: 828 us
  Pallas kernels  288 us (34%)
  waiting for transfers between devices  240 us (29%)
  matrix products  118 us (14%)
  local copies, waits for them, and re-layouts  69.3 us (8%)
  starting transfers between devices  64.1 us (8%)
  other arithmetic  37 us (4%)
  between operations  11 us (1%)
    pallas_call x2, Pallas kernels, place(): pl.pallas_call(functools.partial(place_kernel, masks, pair_rows), out_sha...  288 us
    ppermute x67, waiting for transfers between devices, swap(): return lax.ppermute(x, AXIS, [(i, i ^ mask) for i in range(n)])  240 us
    ppermute x67, starting transfers between devices, swap(): return lax.ppermute(x, AXIS, [(i, i ^ mask) for i in range(n)])  64.1 us
    dot_general x1, matrix products, per_device(): lax.dot_general(exit_grad, w_exit, (((1,), (1,)), ((), ())), preferred_el...  19.2 us
  transfers between devices with their start and end apart: 67, of which 31 were waited for; matrix products, arithmetic and copies ran while one was open for 25% of the time, Pallas kernels for 35%

profile of v1, /device:TPU:0, one launch (start us, length us, event | category | flops | bytes accessed | tf_op | source)
XLA Modules:
  0.0 827.9 jit_solution(8259573687128797681)
XLA Ops:
  31.7 7.7 collective-permute-done.6
  44.6 5.1 collective-permute-done.7
  58.9 7.7 collective-permute-done.8
  68.2 12.5 %collective-permute-done.29.refs_4_ = bf16[2,192,768]{2,1,0:T(8,128)(2,1)} collective-permute-done((bf16[2,192,768]{2,1,0:T(8,128)(2,1)S(1)}, bf16[2,192,768]{2,1,0:T(8,128)(2,1)}, u32[]{:S(2)}, u32[]{:S(2)}) %collective-permute-start.29) | collective-permute-done | bytes 589856 | tf_op jit(solution)/shard_map/ppermute | solution.py:55
  86.2 9.0 %collective-permute-done.20.refs_5_ = bf16[2,48,3072]{2,1,0:T(8,128)(2,1)} collective-permute-done((bf16[2,48,3072]{2,1,0:T(8,128)(2,1)}, bf16[2,48,3072]{2,1,0:T(8,128)(2,1)}, u32[]{:S(2)}, u32[]{:S(2)}) %collective-permute-start.20) | collective-permute-done | bytes 589856 | tf_op jit(solution)/shard_map/ppermute | solution.py:55
  111.9 10.6 %collective-permute-done.31.refs_6_ = bf16[2,192,768]{2,1,0:T(8,128)(2,1)} collective-permute-done((bf16[2,192,768]{2,1,0:T(8,128)(2,1)}, bf16[2,192,768]{2,1,0:T(8,128)(2,1)}, u32[]{:S(2)}, u32[]{:S(2)}) %collective-permute-start.31) | collective-permute-done | bytes 589856 | tf_op jit(solution)/shard_map/ppermute | solution.py:55
  125.6 8.5 %collective-permute-done.22.refs_7_ = bf16[2,48,3072]{2,1,0:T(8,128)(2,1)} collective-permute-done((bf16[2,48,3072]{2,1,0:T(8,128)(2,1)}, bf16[2,48,3072]{2,1,0:T(8,128)(2,1)}, u32[]{:S(2)}, u32[]{:S(2)}) %collective-permute-start.22) | collective-permute-done | bytes 589856 | tf_op jit(solution)/shard_map/ppermute | solution.py:55
  135.4 144.2 %shard_map.331 = bf16[768,3072]{1,0:T(8,128)(2,1)} custom-call(s32[1]{0:T(128)} %bitcast.22.me_ref, bf16[2,48,3072]{2,1,0:T(8,128)(2,1)} %copy-done.23, bf16[2,48,3072]{2,1,0:T(8,128)(2,1)} %collective-permute-done.16.refs_1_, bf16[2,48,3072]{2,1,0:T(8,128)(2,1)} %copy-done.35, bf16[2,48,3072]{2,1,0:T(8,128)(2,1)} %collective-permute-done.18.refs_3_, ...), custom_call_target="tpu_custom_call" | custom-call | tf_op jit(solution)/shard_map/pallas_call | solution.py:114
  280.2 144.2 %shard_map.332 = bf16[3072,768]{1,0:T(8,128)(2,1)} custom-call(s32[1]{0:T(128)} %bitcast.22.me_ref, bf16[2,192,768]{2,1,0:T(8,128)(2,1)} %copy-done.24, bf16[2,192,768]{2,1,0:T(8,128)(2,1)} %copy-done.36, bf16[2,192,768]{2,1,0:T(8,128)(2,1)} %collective-permute-done.27.refs_2_, bf16[2,192,768]{2,1,0:T(8,128)(2,1)} %collective-permute-done.28.refs_3_, ...), custom_call_target="tpu_custom_call" | custom-call | tf_op jit(solution)/shard_map/pallas_call | solution.py:114
  466.3 9.4 %collective-permute-done.11 = bf16[256,768]{1,0:T(8,128)(2,1)} collective-permute-done((bf16[256,768]{1,0:T(8,128)(2,1)}, bf16[256,768]{1,0:T(8,128)(2,1)}, u32[]{:S(2)}, u32[]{:S(2)}) %collective-permute-start.11) | collective-permute-done | bytes 393248 | tf_op jit(solution)/shard_map/ppermute | solution.py:55
  475.7 7.8 collective-permute-done.12
  483.6 13.9 %multiply_convert_fusion = (bf16[1024,3072]{1,0:T(8,128)(2,1)S(1)}, f32[1024,3072]{1,0:T(8,128)}) fusion(f32[3072]{0:T(1024)S(1)} %reshape.580, bf16[768,3072]{1,0:T(8,128)(2,1)} %shard_map.331, bf16[256,768]{1,0:T(8,128)(2,1)} %collective-permute-done.12, bf16[256,768]{1,0:T(8,128)(2,1)} %collective-permute-done.11, ...), kind=kOutput, calls=%fused_computation.11 | convolution fusion | flops 4869586944 | bytes 25178112 | tf_op jit(solution)/shard_map/dot_general | solution.py:292
  497.4 9.6 %add_convert_fusion.2 = bf16[1024,768]{1,0:T(8,128)(2,1)S(1)} fusion(bf16[1024,3072]{1,0:T(8,128)(2,1)S(1)} %get-tuple-element.139, bf16[3072,768]{1,0:T(8,128)(2,1)} %shard_map.332, f32[768]{0:T(1024)S(1)} %fusion.108), kind=kOutput, calls=%fused_computation.26 | convolution fusion | flops 4833411072 | bytes 12585984 | tf_op jit(solution)/shard_map/dot_general | solution.py:294
  512.0 8.6 %collective-permute-done.34 = bf16[256,768]{1,0:T(8,128)(2,1)} collective-permute-done((bf16[256,768]{1,0:T(8,128)(2,1)}, bf16[256,768]{1,0:T(8,128)(2,1)}, u32[]{:S(2)}, u32[]{:S(2)}) %collective-permute-start.34) | collective-permute-done | bytes 393248 | tf_op jit(solution)/shard_map/ppermute | solution.py:55
  520.5 7.6 collective-permute-done.35
  542.0 8.1 convolution_convert_fusion
  554.7 19.2 %convert_reduce_fusion = (bf16[3072]{0:T(1024)(128)(2,1)S(1)}, bf16[1024,3072]{1,0:T(8,128)(2,1)S(1)}) fusion(bf16[3072,768]{1,0:T(8,128)(2,1)} %shard_map.332, bf16[256,768]{1,0:T(8,128)(2,1)} %collective-permute-done.41, bf16[256,768]{1,0:T(8,128)(2,1)} %collective-permute-done.40, bf16[256,768]{1,0:T(8,128)(2,1)} %collective-permute-done.39, ...), kind=kOutput, calls=%fused_computation.10 | convolution fusion | flops 4924634112 | bytes 25188352 | tf_op jit(solution)/shard_map/dot_general | solution.py:298
  573.9 5.1 convolution_convert_fusion.2
  582.0 8.6 %convolution_convert_fusion.1 = bf16[768,3072]{1,0:T(8,128)(2,1)} fusion(bf16[1024,3072]{1,0:T(8,128)(2,1)S(1)} %get-tuple-element.147, bf16[256,768]{1,0:T(8,128)(2,1)} %collective-permute-done.12, bf16[256,768]{1,0:T(8,128)(2,1)} %collective-permute-done.11, bf16[256,768]{1,0:T(8,128)(2,1)} %collective-permute-done.10, bf16[256,768]{1,0:T(8,128)(2,1)S(1)} %copy-done.39), kind=kOutput, calls=%fused_computation.13 | convolution fusion | flops 4840488960 | bytes 12582912 | tf_op jit(solution)/shard_map/dot_general | solution.py:309
  592.6 7.4 collective-permute-done.44
  666.0 56.5 %collective-permute-done.51 = bf16[2,2,1,2,1,48,768]{6,5,4,3,2,1,0:T(8,128)(2,1)S(1)} collective-permute-done((bf16[2,2,1,2,1,48,768]{6,5,4,3,2,1,0:T(8,128)(2,1)S(1)}, bf16[2,2,1,2,1,48,768]{6,5,4,3,2,1,0:T(8,128)(2,1)S(1)}, u32[]{:S(2)}, u32[]{:S(2)}) %collective-permute-start.51) | collective-permute-done | bytes 589856 | tf_op jit(solution)/shard_map/ppermute | solution.py:55
  749.5 5.3 collective-permute-done.49
  768.0 33.1 %collective-permute-done.63 = bf16[1,2,1,1,2,96,768]{6,5,4,3,2,1,0:T(8,128)(2,1)S(1)} collective-permute-done((bf16[1,2,1,1,2,96,768]{6,5,4,3,2,1,0:T(8,128)(2,1)S(1)}, bf16[1,2,1,1,2,96,768]{6,5,4,3,2,1,0:T(8,128)(2,1)S(1)}, u32[]{:S(2)}, u32[]{:S(2)}) %collective-permute-start.63) | collective-permute-done | bytes 589856 | tf_op jit(solution)/shard_map/ppermute | solution.py:55
  803.3 10.5 %collective-permute-done.57 = bf16[1,2,1,1,2,24,3072]{6,5,4,3,2,1,0:T(8,128)(2,1)S(1)} collective-permute-done((bf16[1,2,1,1,2,24,3072]{6,5,4,3,2,1,0:T(8,128)(2,1)S(1)}, bf16[1,2,1,1,2,24,3072]{6,5,4,3,2,1,0:T(8,128)(2,1)S(1)}, u32[]{:S(2)}, u32[]{:S(2)}) %collective-permute-start.57) | collective-permute-done | bytes 589856 | tf_op jit(solution)/shard_map/ppermute | solution.py:55
  (531 shorter events, 256.8 us)
Async XLA Ops:
  25.4 29.2 %collective-permute-start.19 = (bf16[2,48,3072]{2,1,0:T(8,128)(2,1)S(1)}, bf16[2,48,3072]{2,1,0:T(8,128)(2,1)}, u32[]{:S(2)}, u32[]{:S(2)}) collective-permute-start(bf16[2,48,3072]{2,1,0:T(8,128)(2,1)S(1)} %pad_maximum_fusion.8.refs_0_), channel_id=1, source_target_pairs={{0,16},{1,17},{2,18},{3,19},{4,20},{5,21},{6,22},{7,23},{8,24},{9,... | collective-permute-start | bytes 1769480 | tf_op jit(solution)/shard_map/ppermute | solution.py:55
  28.4 27.7 %collective-permute-start.16 = (bf16[2,48,3072]{2,1,0:T(8,128)(2,1)S(1)}, bf16[2,48,3072]{2,1,0:T(8,128)(2,1)}, u32[]{:S(2)}, u32[]{:S(2)}) collective-permute-start(bf16[2,48,3072]{2,1,0:T(8,128)(2,1)S(1)} %pad_maximum_fusion.8.refs_0_), channel_id=1, source_target_pairs={{0,2},{1,3},{2,0},{3,1},{4,6},{5,7},{6,4},{7,5},{8,10},{9,11},{10,... | collective-permute-start | bytes 1769480 | tf_op jit(solution)/shard_map/ppermute | solution.py:55
  30.1 27.7 %collective-permute-start.17 = (bf16[2,48,3072]{2,1,0:T(8,128)(2,1)S(1)}, bf16[2,48,3072]{2,1,0:T(8,128)(2,1)S(1)}, u32[]{:S(2)}, u32[]{:S(2)}) collective-permute-start(bf16[2,48,3072]{2,1,0:T(8,128)(2,1)S(1)} %pad_maximum_fusion.8.refs_0_), channel_id=1, source_target_pairs={{0,4},{1,5},{2,6},{3,7},{4,0},{5,1},{6,2},{7,3},{8,12},{9,13},{10,... | collective-permute-start | bytes 1769480 | tf_op jit(solution)/shard_map/ppermute | solution.py:55
  66.5 28.7 %collective-permute-start.20 = (bf16[2,48,3072]{2,1,0:T(8,128)(2,1)}, bf16[2,48,3072]{2,1,0:T(8,128)(2,1)}, u32[]{:S(2)}, u32[]{:S(2)}) collective-permute-start(bf16[2,48,3072]{2,1,0:T(8,128)(2,1)} %collective-permute-done.19.refs_4_), channel_id=1, source_target_pairs={{0,2},{1,3},{2,0},{3,1},{4,6},{5,7},{6,4},{7,5},{8,10},{9,11},{10,... | collective-permute-start | bytes 1769480 | tf_op jit(solution)/shard_map/ppermute | solution.py:55
  80.7 30.2 %collective-permute-start.21 = (bf16[2,48,3072]{2,1,0:T(8,128)(2,1)}, bf16[2,48,3072]{2,1,0:T(8,128)(2,1)}, u32[]{:S(2)}, u32[]{:S(2)}) collective-permute-start(bf16[2,48,3072]{2,1,0:T(8,128)(2,1)} %collective-permute-done.19.refs_4_), channel_id=1, source_target_pairs={{0,4},{1,5},{2,6},{3,7},{4,0},{5,1},{6,2},{7,3},{8,12},{9,13},{10,... | collective-permute-start | bytes 1769480 | tf_op jit(solution)/shard_map/ppermute | solution.py:55
  82.2 27.6 %collective-permute-start.18 = (bf16[2,48,3072]{2,1,0:T(8,128)(2,1)}, bf16[2,48,3072]{2,1,0:T(8,128)(2,1)}, u32[]{:S(2)}, u32[]{:S(2)}) collective-permute-start(bf16[2,48,3072]{2,1,0:T(8,128)(2,1)} %collective-permute-done.16.refs_1_), channel_id=1, source_target_pairs={{0,4},{1,5},{2,6},{3,7},{4,0},{5,1},{6,2},{7,3},{8,12},{9,13},{10,... | collective-permute-start | bytes 1769480 | tf_op jit(solution)/shard_map/ppermute | solution.py:55
  82.7 39.7 %collective-permute-start.31 = (bf16[2,192,768]{2,1,0:T(8,128)(2,1)}, bf16[2,192,768]{2,1,0:T(8,128)(2,1)}, u32[]{:S(2)}, u32[]{:S(2)}) collective-permute-start(bf16[2,192,768]{2,1,0:T(8,128)(2,1)} %collective-permute-done.29.refs_4_), channel_id=1, source_target_pairs={{0,4},{1,5},{2,6},{3,7},{4,0},{5,1},{6,2},{7,3},{8,12},{9,13},{10,... | collective-permute-start | bytes 1769480 | tf_op jit(solution)/shard_map/ppermute | solution.py:55
  86.2 338.2 %collective-permute-start.9 = (bf16[2,2,2,2,1,48,768]{6,5,4,3,2,1,0:T(8,128)(2,1)}, bf16[2,2,2,2,1,48,768]{6,5,4,3,2,1,0:T(8,128)(2,1)}, u32[]{:S(2)}, u32[]{:S(2)}) collective-permute-start(bf16[2,2,2,2,1,48,768]{6,5,4,3,2,1,0:T(8,128)(2,1)} %pad_maximum_fusion.5), channel_id=1, source_target_pairs={{0,1},{1,0},{2,3},{3,2},{4,5},{5,4},{6,7},{7,6},{8,9},{9,8},{10,11... | collective-permute-start | bytes 3538952 | tf_op jit(solution)/shard_map/ppermute | solution.py:55
  95.2 39.0 %collective-permute-start.22 = (bf16[2,48,3072]{2,1,0:T(8,128)(2,1)}, bf16[2,48,3072]{2,1,0:T(8,128)(2,1)}, u32[]{:S(2)}, u32[]{:S(2)}) collective-permute-start(bf16[2,48,3072]{2,1,0:T(8,128)(2,1)} %collective-permute-done.20.refs_5_), channel_id=1, source_target_pairs={{0,4},{1,5},{2,6},{3,7},{4,0},{5,1},{6,2},{7,3},{8,12},{9,13},{10,... | collective-permute-start | bytes 1769480 | tf_op jit(solution)/shard_map/ppermute | solution.py:55
  109.8 170.3 %collective-permute-start.30 = (bf16[2,192,768]{2,1,0:T(8,128)(2,1)}, bf16[2,192,768]{2,1,0:T(8,128)(2,1)}, u32[]{:S(2)}, u32[]{:S(2)}) collective-permute-start(bf16[2,192,768]{2,1,0:T(8,128)(2,1)} %collective-permute-done.29.refs_4_), channel_id=1, source_target_pairs={{0,2},{1,3},{2,0},{3,1},{4,6},{5,7},{6,4},{7,5},{8,10},{9,11},{10,... | collective-permute-start | bytes 1769480 | tf_op jit(solution)/shard_map/ppermute | solution.py:55
  110.9 168.7 %collective-permute-start.28 = (bf16[2,192,768]{2,1,0:T(8,128)(2,1)}, bf16[2,192,768]{2,1,0:T(8,128)(2,1)}, u32[]{:S(2)}, u32[]{:S(2)}) collective-permute-start(bf16[2,192,768]{2,1,0:T(8,128)(2,1)} %collective-permute-done.27.refs_2_), channel_id=1, source_target_pairs={{0,2},{1,3},{2,0},{3,1},{4,6},{5,7},{6,4},{7,5},{8,10},{9,11},{10,... | collective-permute-start | bytes 1769480 | tf_op jit(solution)/shard_map/ppermute | solution.py:55
  122.5 157.7 %collective-permute-start.32 = (bf16[2,192,768]{2,1,0:T(8,128)(2,1)}, bf16[2,192,768]{2,1,0:T(8,128)(2,1)}, u32[]{:S(2)}, u32[]{:S(2)}) collective-permute-start(bf16[2,192,768]{2,1,0:T(8,128)(2,1)} %collective-permute-done.31.refs_6_), channel_id=1, source_target_pairs={{0,2},{1,3},{2,0},{3,1},{4,6},{5,7},{6,4},{7,5},{8,10},{9,11},{10,... | collective-permute-start | bytes 1769480 | tf_op jit(solution)/shard_map/ppermute | solution.py:55
  134.2 293.0 %collective-permute-start.4 = (bf16[2,2,2,2,1,49,768]{6,3,5,4,2,1,0:T(2,128)(2,1)}, bf16[2,2,2,2,1,49,768]{6,3,5,4,2,1,0:T(2,128)(2,1)}, u32[]{:S(2)}, u32[]{:S(2)}) collective-permute-start(bf16[2,2,2,2,1,49,768]{6,3,5,4,2,1,0:T(2,128)(2,1)} %copy.228), channel_id=1, source_target_pairs={{0,1},{1,0},{2,3},{3,2},{4,5},{5,4},{6,7},{7,6},{8,9},{9,8},{10,11... | collective-permute-start | bytes 3612680 | tf_op jit(solution)/shard_map/ppermute | solution.py:55
  279.6 262.4 %collective-permute-start.39 = (bf16[256,768]{1,0:T(8,128)(2,1)}, bf16[256,768]{1,0:T(8,128)(2,1)}, u32[]{:S(2)}, u32[]{:S(2)}) collective-permute-start(bf16[256,768]{1,0:T(8,128)(2,1)} %get-tuple-element.56), channel_id=1, source_target_pairs={{0,1},{1,0},{2,3},{3,2},{4,5},{5,4},{6,7},{7,6},{8,9},{9,8},{10,11... | collective-permute-start | bytes 1179656 | tf_op jit(solution)/shard_map/ppermute | solution.py:55
  280.2 261.8 %collective-permute-start.40 = (bf16[256,768]{1,0:T(8,128)(2,1)}, bf16[256,768]{1,0:T(8,128)(2,1)}, u32[]{:S(2)}, u32[]{:S(2)}) collective-permute-start(bf16[256,768]{1,0:T(8,128)(2,1)} %get-tuple-element.55), channel_id=1, source_target_pairs={{0,8},{1,9},{2,10},{3,11},{4,12},{5,13},{6,14},{7,15},{8,0},{9,1},... | collective-permute-start | bytes 1179656 | tf_op jit(solution)/shard_map/ppermute | solution.py:55
  510.3 31.7 %collective-permute-start.41 = (bf16[256,768]{1,0:T(8,128)(2,1)}, bf16[256,768]{1,0:T(8,128)(2,1)}, u32[]{:S(2)}, u32[]{:S(2)}) collective-permute-start(bf16[256,768]{1,0:T(8,128)(2,1)} %get-tuple-element.54), channel_id=1, source_target_pairs={{0,9},{1,8},{2,11},{3,10},{4,13},{5,12},{6,15},{7,14},{8,1},{9,0},... | collective-permute-start | bytes 1179656 | tf_op jit(solution)/shard_map/ppermute | solution.py:55
  553.6 174.5 %collective-permute-start.61 = (bf16[2,2,2,1,2,96,768]{6,5,4,3,2,1,0:T(8,128)(2,1)}, bf16[2,2,2,1,2,96,768]{6,5,4,3,2,1,0:T(8,128)(2,1)}, u32[]{:S(2)}, u32[]{:S(2)}) collective-permute-start(bf16[2,2,2,1,2,96,768]{6,5,4,3,2,1,0:T(8,128)(2,1)} %constant_dynamic-slice_fusion.2), channel_id=1, source_target_pairs={{0,2},{1,3},{2,0},{3,1},{4,6},{5,7},{6,4},{7,5},{8,10},{9,11},{10,... | collective-permute-start | bytes 7077896 | tf_op jit(solution)/shard_map/ppermute | solution.py:55
  656.4 74.8 %collective-permute-start.55 = (bf16[2,2,1,2,2,24,3072]{6,5,4,3,2,1,0:T(8,128)(2,1)S(1)}, bf16[2,2,1,2,2,24,3072]{6,5,4,3,2,1,0:T(8,128)(2,1)S(1)}, u32[]{:S(2)}, u32[]{:S(2)}) collective-permute-start(bf16[2,2,1,2,2,24,3072]{6,5,4,3,2,1,0:T(8,128)(2,1)S(1)} %constant_dynamic-slice_fusion.5), channel_id=1, source_target_pairs={{0,4},{1,5},{2,6},{3,7},{4,0},{5,1},{6,2},{7,3},{8,12},{9,13},{10,... | collective-permute-start | bytes 7077896 | tf_op jit(solution)/shard_map/ppermute | solution.py:55
  659.6 62.9 %collective-permute-start.51 = (bf16[2,2,1,2,1,48,768]{6,5,4,3,2,1,0:T(8,128)(2,1)S(1)}, bf16[2,2,1,2,1,48,768]{6,5,4,3,2,1,0:T(8,128)(2,1)S(1)}, u32[]{:S(2)}, u32[]{:S(2)}) collective-permute-start(bf16[2,2,1,2,1,48,768]{6,5,4,3,2,1,0:T(8,128)(2,1)S(1)} %constant_dynamic-slice_fusion.9), channel_id=1, source_target_pairs={{0,4},{1,5},{2,6},{3,7},{4,0},{5,1},{6,2},{7,3},{8,12},{9,13},{10,... | collective-permute-start | bytes 1769480 | tf_op jit(solution)/shard_map/ppermute | solution.py:55
  663.5 60.3 %collective-permute-start.46 = (bf16[2,2,2,1,1,49,768]{6,2,5,4,3,1,0:T(2,128)(2,1)S(1)}, bf16[2,2,2,1,1,49,768]{6,2,5,4,3,1,0:T(2,128)(2,1)S(1)}, u32[]{:S(2)}, u32[]{:S(2)}) collective-permute-start(bf16[2,2,2,1,1,49,768]{6,2,5,4,3,1,0:T(2,128)(2,1)S(1)} %copy.258), channel_id=1, source_target_pairs={{0,2},{1,3},{2,0},{3,1},{4,6},{5,7},{6,4},{7,5},{8,10},{9,11},{10,... | collective-permute-start | bytes 1806344 | tf_op jit(solution)/shard_map/ppermute | solution.py:55
  730.6 29.5 %collective-permute-start.62 = (bf16[2,2,1,1,2,96,768]{6,5,4,3,2,1,0:T(8,128)(2,1)S(1)}, bf16[2,2,1,1,2,96,768]{6,5,4,3,2,1,0:T(8,128)(2,1)}, u32[]{:S(2)}, u32[]{:S(2)}) collective-permute-start(bf16[2,2,1,1,2,96,768]{6,5,4,3,2,1,0:T(8,128)(2,1)S(1)} %constant_dynamic-slice_fusion.1), channel_id=1, source_target_pairs={{0,4},{1,5},{2,6},{3,7},{4,0},{5,1},{6,2},{7,3},{8,12},{9,13},{10,... | collective-permute-start | bytes 3538952 | tf_op jit(solution)/shard_map/ppermute | solution.py:55
  733.4 29.0 %collective-permute-start.56 = (bf16[2,2,1,1,2,24,3072]{6,5,4,3,2,1,0:T(8,128)(2,1)}, bf16[2,2,1,1,2,24,3072]{6,5,4,3,2,1,0:T(8,128)(2,1)}, u32[]{:S(2)}, u32[]{:S(2)}) collective-permute-start(bf16[2,2,1,1,2,24,3072]{6,5,4,3,2,1,0:T(8,128)(2,1)} %constant_dynamic-slice_fusion.4), channel_id=1, source_target_pairs={{0,2},{1,3},{2,0},{3,1},{4,6},{5,7},{6,4},{7,5},{8,10},{9,11},{10,... | collective-permute-start | bytes 3538952 | tf_op jit(solution)/shard_map/ppermute | solution.py:55
  761.7 39.4 %collective-permute-start.63 = (bf16[1,2,1,1,2,96,768]{6,5,4,3,2,1,0:T(8,128)(2,1)S(1)}, bf16[1,2,1,1,2,96,768]{6,5,4,3,2,1,0:T(8,128)(2,1)S(1)}, u32[]{:S(2)}, u32[]{:S(2)}) collective-permute-start(bf16[1,2,1,1,2,96,768]{6,5,4,3,2,1,0:T(8,128)(2,1)S(1)} %constant_dynamic-slice_fusion), channel_id=1, source_target_pairs={{0,16},{1,17},{2,18},{3,19},{4,20},{5,21},{6,22},{7,23},{8,24},{9,... | collective-permute-start | bytes 1769480 | tf_op jit(solution)/shard_map/ppermute | solution.py:55
  764.1 49.7 %collective-permute-start.57 = (bf16[1,2,1,1,2,24,3072]{6,5,4,3,2,1,0:T(8,128)(2,1)S(1)}, bf16[1,2,1,1,2,24,3072]{6,5,4,3,2,1,0:T(8,128)(2,1)S(1)}, u32[]{:S(2)}, u32[]{:S(2)}) collective-permute-start(bf16[1,2,1,1,2,24,3072]{6,5,4,3,2,1,0:T(8,128)(2,1)S(1)} %constant_dynamic-slice_fusion.3), channel_id=1, source_target_pairs={{0,16},{1,17},{2,18},{3,19},{4,20},{5,21},{6,22},{7,23},{8,24},{9,... | collective-permute-start | bytes 1769480 | tf_op jit(solution)/shard_map/ppermute | solution.py:55
  (135 other events, 1808.9 us)
